TPU v7x, 32 devices: a whole 2x2x4 slice. The times are simulated.
32 devices in a mesh: frame: 4 (over y, x), pos: 8 (over z, core).
Axes of the slice: x: 2, y: 2, z: 4, core: 2. Of those that a mesh axis runs over, the one named last changes fastest.
Arguments:
- frames_in: bfloat16 [256, 256, 512], P('frame', 'pos'), may hold values from -40 to 40
- attn_gain: float32 [512], replicated, may hold values from 0.5 to 1.5
- w_query: bfloat16 [512, 512], replicated, may hold values from -4 to 4
- w_key: bfloat16 [512, 512], replicated, may hold values from -4 to 4
- w_value: bfloat16 [512, 512], replicated, may hold values from -0.25 to 0.25
- w_output: bfloat16 [512, 512], replicated, may hold values from -0.25 to 0.25
- moe_gain: float32 [512], replicated, may hold values from 0.5 to 1.5
- dispatch_keys: bfloat16 [512, 1024], replicated, may hold values from -10 to 10
- w_in: bfloat16 [16, 512, 2048], P('pos'), may hold values from -0.25 to 0.25
- w_out: bfloat16 [16, 2048, 512], P('pos'), may hold values from -0.125 to 0.125
Outputs:
- frames_out: bfloat16 [256, 256, 512], P('frame', 'pos')
All inputs are finite; a program needn't handle non-finite values.
Results may differ from a plain program's by a relative error of at most 0.0052.
Values may be sent and summed in bfloat16 or wider, within the bound.
A program may use at most 64 MiB of HBM per device.

v0:
```python
import jax
import jax.numpy as jnp
from jax import lax
from jax.sharding import PartitionSpec as P

HEADS = 8
EXPERTS = 16
SLOTS = 64


EPS = 1e-06
LOGIT_SCALE = 3.0
MASKED = -1e30


def joined(shard, axis, combine):
    everything = jax.tree.map(lambda part: lax.all_gather(part, axis), shard)
    leading = jax.tree.map(lambda part: part[0], everything)

    def hop(k, so_far):
        return combine(so_far, jax.tree.map(lambda part: part[k], everything))

    return lax.fori_loop(1, lax.axis_size(axis), hop, leading)


def from_partner(block, axis, apart):
    count = lax.axis_size(axis)
    route = []
    for low in range(count):
        high = low | 1 << apart
        if high != low and high < count:
            route += [(low, high), (high, low)]
    return lax.ppermute(block, axis, route)


def rms_scale(values_in, gain):
    values_in = values_in.astype(jnp.float32)
    mean_sq = jnp.mean(values_in * values_in, axis=-1, keepdims=True)
    return values_in * lax.rsqrt(mean_sq + EPS) * gain


def project(rows_in, weights):
    return jnp.dot(rows_in, weights, preferred_element_type=jnp.float32).astype(jnp.bfloat16)


def softmax_rows(scores, axis_index):
    largest = jnp.max(scores, axis=axis_index, keepdims=True)
    weights = jnp.exp(scores - largest)
    return (weights / jnp.sum(weights, axis=axis_index, keepdims=True)).astype(jnp.bfloat16)


def attend(queries, keys_block, values_block):
    frame_count = queries.shape[0]
    score_scale = queries.shape[3] ** (-0.5)
    causal = jnp.arange(frame_count)[:, None] >= jnp.arange(frame_count)[None, :]

    def one_head(triple):
        queries_head, keys_head, values_head = triple
        scores = (
            jnp.einsum("fpd,gpd->pfg", queries_head, keys_head, preferred_element_type=jnp.float32)
            * score_scale
        )
        scores = jnp.where(causal[None], scores, MASKED)
        attention = softmax_rows(scores, 2)
        return jnp.einsum(
            "pfg,gpd->fpd", attention, values_head, preferred_element_type=jnp.float32
        ).astype(jnp.bfloat16)

    by_head = tuple(
        (jnp.moveaxis(array_in, 2, 0) for array_in in (queries, keys_block, values_block))
    )
    return jnp.moveaxis(lax.map(one_head, by_head), 0, 2)


def merge_stats(first_pair, second_pair):
    largest = jnp.maximum(first_pair[0], second_pair[0])
    totals = first_pair[1] * jnp.exp(first_pair[0] - largest) + second_pair[1] * jnp.exp(
        second_pair[0] - largest
    )
    return (largest, totals)


def local(
    frames_in, attn_gain, w_query, w_key, w_value, w_output, moe_gain, dispatch_keys, w_in, w_out
):
    frame_count, pos_count, features = frames_in.shape
    head_dim = features // HEADS
    normed = rms_scale(frames_in, attn_gain).astype(jnp.bfloat16)
    spread = lax.all_to_all(normed, "frame", split_axis=1, concat_axis=0, tiled=True)
    all_frames = spread.shape[0]
    pos_part = spread.shape[1]
    flattened = spread.reshape(all_frames * pos_part, features)
    shaped = (all_frames, pos_part, HEADS, head_dim)
    queries = project(flattened, w_query).reshape(shaped)
    keys_block = project(flattened, w_key).reshape(shaped)
    values_block = project(flattened, w_value).reshape(shaped)
    mixed_part = attend(queries, keys_block, values_block).reshape(all_frames, pos_part, features)
    mixed_heads = lax.all_to_all(mixed_part, "frame", split_axis=0, concat_axis=1, tiled=True)
    mixed_heads = mixed_heads.reshape(frame_count * pos_count, features)
    residual = (
        frames_in.reshape(frame_count * pos_count, features).astype(jnp.float32)
        + jnp.dot(mixed_heads, w_output, preferred_element_type=jnp.float32)
    ).astype(jnp.bfloat16)
    moe_input = rms_scale(residual, moe_gain).astype(jnp.bfloat16)
    logits = LOGIT_SCALE * jnp.dot(moe_input, dispatch_keys, preferred_element_type=jnp.float32)
    local_max = jnp.max(logits, axis=0)
    local_sum = jnp.sum(jnp.exp(logits - local_max[None, :]), axis=0)
    largest, totals = joined((local_max, local_sum), "pos", merge_stats)
    dispatch = (jnp.exp(logits - largest[None, :]) / totals[None, :]).astype(jnp.bfloat16)
    count_pos = lax.axis_size("pos")
    position = lax.axis_index("pos")
    splits = max(1, count_pos // EXPERTS)
    split_bits = splits.bit_length() - 1
    pieces_dev = EXPERTS * splits // count_pos
    local_experts = max(1, pieces_dev // splits)
    slot_partial = lax.dot_general(
        dispatch, moe_input, (((0,), (0,)), ((), ())), preferred_element_type=jnp.float32
    )
    slot_totals = lax.psum(slot_partial.astype(jnp.bfloat16), "pos").astype(jnp.float32)
    first_row = position * pieces_dev // splits * SLOTS
    slot_in = lax.dynamic_slice_in_dim(slot_totals, first_row, local_experts * SLOTS, 0).astype(
        jnp.bfloat16
    )
    slot_in = slot_in.reshape(local_experts, SLOTS, features)
    hidden = jax.nn.gelu(
        jnp.einsum("esd,edh->esh", slot_in, w_in, preferred_element_type=jnp.float32)
    ).astype(jnp.bfloat16)
    partial_out = jnp.einsum(
        "esh,ehd->esd", hidden, w_out, preferred_element_type=jnp.float32
    ).astype(jnp.bfloat16)
    shares = partial_out.astype(jnp.float32).reshape(pieces_dev * SLOTS, features)
    for bit_index in reversed(range(split_bits)):
        half_rows = shares.shape[0] // 2
        lower_half = shares[:half_rows]
        upper_half = shares[half_rows:]
        upper_bit = position // 2**bit_index % 2 == 1
        kept_rows = jnp.where(upper_bit, upper_half, lower_half)
        sent_rows = jnp.where(upper_bit, lower_half, upper_half)
        shares = kept_rows + from_partner(sent_rows.astype(jnp.bfloat16), "pos", bit_index).astype(
            sent_rows.dtype
        )
    outputs = shares.astype(jnp.bfloat16)
    combine = softmax_rows(logits, 1)
    moe_out = jnp.dot(
        combine,
        lax.all_gather(outputs, "pos", axis=0, tiled=True),
        preferred_element_type=jnp.float32,
    )
    frames_out = (residual.astype(jnp.float32) + moe_out).astype(jnp.bfloat16)
    return frames_out.reshape(frame_count, pos_count, features)


def solution(mesh):
    in_specs = (
        P("frame", "pos", None),
        P(),
        P(),
        P(),
        P(),
        P(),
        P(),
        P(),
        P("pos", None, None),
        P("pos", None, None),
    )
    out_specs = P("frame", "pos", None)
    return jax.shard_map(local, mesh=mesh, in_specs=in_specs, out_specs=out_specs, check_vma=False)
```

profile of v0, /device:TPU:9, one launch (start us, length us, event | category | flops | bytes accessed | tf_op | source)
XLA Modules:
  0.0 316.4 jit_solution(14062341687904895166)
XLA Ops:
  6.5 3.8 %multiply_reduce_fusion.2 = f32[64,32]{0,1:T(8,128)S(1)} fusion(bf16[64,32,512]{2,1,0:T(8,128)(2,1)} %param.14), kind=kLoop, calls=%fused_computation.45 | loop fusion | flops 3143680 | bytes 2105344 | tf_op jit(solution)/shard_map/reduce_sum | solution.py:38
  10.3 4.2 %multiply_convert_fusion = bf16[64,32,512]{2,0,1:T(8,128)(2,1)} fusion(f32[512]{0:T(512)} %param.15, f32[64,32]{0,1:T(8,128)S(1)} %add_rsqrt_fusion, bf16[64,32,512]{2,1,0:T(8,128)(2,1)} %param.14), kind=kLoop, calls=%fused_computation.44 | loop fusion | flops 4194304 | bytes 4204544 | tf_op jit(solution)/shard_map/convert_element_type | solution.py:88
  14.6 3.8 %all-to-all-start = ((bf16[64,32,512]{2,0,1:T(8,128)(2,1)}), bf16[64,32,512]{2,0,1:T(8,128)(2,1)S(1)}, u32[]{:S(2)}, u32[]{:S(2)}) async-start(bf16[64,32,512]{2,0,1:T(8,128)(2,1)} %multiply_convert_fusion), calls=%async_computation | async-start | bytes 4194304 | tf_op jit(solution)/shard_map/all_to_all | solution.py:89
  18.4 24.1 %all-to-all-done = bf16[64,32,512]{2,0,1:T(8,128)(2,1)S(1)} async-done(((bf16[64,32,512]{2,0,1:T(8,128)(2,1)}), bf16[64,32,512]{2,0,1:T(8,128)(2,1)S(1)}, u32[]{:S(2)}, u32[]{:S(2)}) %all-to-all-start) | async-done | bytes 2097184 | tf_op jit(solution)/shard_map/all_to_all | solution.py:89
  46.2 3.6 %reshape.60 = bf16[256,8,8,64]{3,2,1,0:T(8,128)(2,1)} reshape(bf16[2048,512]{1,0:T(8,128)(2,1)S(1)} %convolution_convert_fusion.1) | data formatting | bytes 4194304 | tf_op jit(solution)/shard_map/reshape | solution.py:95
  49.9 5.0 %copy.36 = bf16[8,256,8,64]{1,3,2,0:T(8,128)(2,1)S(1)} copy(bf16[8,256,8,64]{3,0,2,1:T(8,128)(2,1)} %bitcast.81) | data formatting | bytes 4194304
  54.9 4.4 %convolution_convert_fusion.2 = bf16[2048,512]{1,0:T(8,128)(2,1)} fusion(bf16[2048,512]{1,0:T(8,128)(2,1)} %bitcast.88, bf16[512,512]{1,0:T(8,128)(2,1)} %param.16), kind=kOutput, calls=%fused_computation.49 | convolution fusion | flops 1074790400 | bytes 4718592 | tf_op jit(solution)/shard_map/dot_general | solution.py:43
  61.9 6.2 %reshape.58 = bf16[256,8,8,64]{3,2,1,0:T(8,128)(2,1)} reshape(bf16[2048,512]{1,0:T(8,128)(2,1)} %convolution_convert_fusion.3) | data formatting | bytes 4194304 | tf_op jit(solution)/shard_map/reshape | solution.py:96
  68.0 5.9 %copy.34 = bf16[8,256,8,64]{1,3,2,0:T(8,128)(2,1)} copy(bf16[8,256,8,64]{3,0,2,1:T(8,128)(2,1)} %bitcast.82) | data formatting | bytes 4194304
  73.9 6.2 %reshape.59 = bf16[256,8,8,64]{3,2,1,0:T(8,128)(2,1)} reshape(bf16[2048,512]{1,0:T(8,128)(2,1)} %convolution_convert_fusion.2) | data formatting | bytes 4194304 | tf_op jit(solution)/shard_map/reshape | solution.py:94
  80.1 5.9 %copy.35 = bf16[8,256,8,64]{1,3,2,0:T(8,128)(2,1)} copy(bf16[8,256,8,64]{3,0,2,1:T(8,128)(2,1)} %bitcast.83) | data formatting | bytes 4194304
  86.0 47.0 %while.29 = (s32[]{:T(128)}, bf16[8,256,8,64]{1,3,0,2:T(8,128)(2,1)}, bf16[8,256,8,64]{1,3,2,0:T(8,128)(2,1)}, bf16[8,256,8,64]{1,3,2,0:T(8,128)(2,1)}, bf16[8,256,8,64]{1,3,2,0:T(8,128)(2,1)S(1)}, /*index=5*/s32[]{:T(128)}) while((s32[]{:T(128)}, bf16[8,256,8,64]{1,3,0,2:T(8,128)(2,1)}, bf16[8,256,8,64]{1,3,2,0:T(8,128)(2,1)}, ...), condition=%wide.region_4.5_spmd.clone, body=%wide.region_1.4_spmd.clone.sunk | while | flops 137560320 | bytes 5392461 | solution.py:72
  127.1 3.1 fusion.93
  133.0 4.7 %copy.38 = bf16[256,8,512]{2,1,0:T(8,128)(2,1)} copy(bf16[256,8,512]{0,2,1:T(8,128)(2,1)} %bitcast.86) | data formatting | bytes 4194304 | tf_op jit(solution)/shard_map/reshape | solution.py:97
  137.7 4.4 %all-to-all-start.1 = ((bf16[256,8,512]{2,1,0:T(8,128)(2,1)}), bf16[256,8,512]{2,1,0:T(8,128)(2,1)}, u32[]{:S(2)}, u32[]{:S(2)}) async-start(bf16[256,8,512]{2,1,0:T(8,128)(2,1)} %copy.38), calls=%async_computation.1 | async-start | bytes 4194304 | tf_op jit(solution)/shard_map/all_to_all | solution.py:98
  143.7 4.4 %copy.31 = f32[64,32,512]{2,1,0:T(8,128)} copy(f32[64,32,512]{2,0,1:T(8,128)S(1)} %copy_convert_fusion) | data formatting | bytes 8388608 | tf_op jit(solution)/shard_map/convert_element_type | solution.py:101
  148.0 18.5 %all-to-all-done.1 = bf16[256,8,512]{2,1,0:T(8,128)(2,1)} async-done(((bf16[256,8,512]{2,1,0:T(8,128)(2,1)}), bf16[256,8,512]{2,1,0:T(8,128)(2,1)}, u32[]{:S(2)}, u32[]{:S(2)}) %all-to-all-start.1) | async-done | bytes 2097184 | tf_op jit(solution)/shard_map/all_to_all | solution.py:98
  179.1 15.5 %all-gather = f32[8192]{0:T(1024)S(1)} all-gather(f32[1024]{0:T(1024)S(1)} %get-tuple-element.201), channel_id=2, replica_groups=mesh['frame'=4,'pos'=8] {'pos'}, dimensions={0}, use_global_device_ids=true | all-gather | bytes 36864 | tf_op jit(solution)/shard_map/all_gather | solution.py:17
  194.6 14.2 %all-gather.1 = f32[8192]{0:T(1024)S(1)} all-gather(f32[1024]{0:T(1024)S(1)} %exponential_reduce_fusion), channel_id=3, replica_groups=mesh['frame'=4,'pos'=8] {'pos'}, dimensions={0}, use_global_device_ids=true | all-gather | bytes 36864 | tf_op jit(solution)/shard_map/all_gather | solution.py:17
  209.2 6.9 %fusion.42 = bf16[1024,512]{1,0:T(8,128)(2,1)} fusion(f32[2048,1024]{1,0:T(8,128)} %copy-done.2, f32[1024]{0:T(1024)S(1)} %get-tuple-element.172, f32[1024]{0:T(1024)S(1)} %get-tuple-element.171, bf16[2048,512]{1,0:T(8,128)(2,1)S(1)} %get-tuple-element.229, f32[512]{0:T(512)S(1)} %copy-done.9, f32[2048]{0:T(1024)S(1)} %add_rsqrt_fusion.1), kind=kOutput, calls=%fused_computation.53 | convolution fusion | flops 2160590848 | bytes 11552768 | tf_op jit(solution)/shard_map/dot_general | solution.py:116
  216.2 56.1 %all-reduce.2.cloned.1.call-done = bf16[1024,512]{1,0:T(8,128)(2,1)} async-done(((bf16[1024,512]{1,0:T(8,128)(2,1)}), bf16[1024,512]{1,0:T(8,128)(2,1)}) %all-reduce.2.cloned.1.call-update) | async-done | bytes 1048592 | tf_op jit(solution)/shard_map/psum | solution.py:119
  273.2 5.9 %convolution_convert_fusion.4 = bf16[2,64,512]{2,1,0:T(8,128)(2,1)} fusion(bf16[2,2048,512]{2,1,0:T(8,128)(2,1)} %param.23, bf16[2,64,512]{2,1,0:T(8,128)(2,1)S(1)} %bitcast.91, bf16[2,512,2048]{2,1,0:T(8,128)(2,1)} %param.22), kind=kOutput, calls=%fused_computation.54 | convolution fusion | flops 539295744 | bytes 8650752 | tf_op jit(solution)/shard_map/esh,ehd->esd/dot_general | solution.py:128
  279.2 24.1 %all-gather.4.cloned.1.call-done = bf16[1024,512]{1,0:T(8,128)(2,1)} async-done(((bf16[128,512]{1,0:T(8,128)(2,1)}), bf16[1024,512]{1,0:T(8,128)(2,1)}) %all-gather.4.cloned.1.call-update) | async-done | bytes 1048592 | tf_op jit(solution)/shard_map/all_gather | solution.py:146
  303.3 6.2 %fusion.38 = bf16[2048,512]{1,0:T(8,128)(2,1)} fusion(bf16[2048,512]{1,0:T(8,128)(2,1)S(1)} %get-tuple-element.229, bf16[1024,512]{1,0:T(8,128)(2,1)} %all-gather.4.cloned.1.call-done, f32[2048,1024]{1,0:T(8,128)} %copy-done.2, f32[2048]{0:T(1024)S(1)} %get-tuple-element.200, f32[2048]{0:T(1024)S(1)} %get-tuple-element.230), kind=kOutput, calls=%fused_computation.41 | convolution fusion | flops 2159017984 | bytes 13647872 | tf_op jit(solution)/shard_map/dot_general | solution.py:144
  (79 shorter events, 65.7 us)
Async XLA Ops:
  6.5 165.3 %copy-start = (bf16[512,1024]{1,0:T(8,128)(2,1)S(1)}, bf16[512,1024]{1,0:T(8,128)(2,1)}, u32[]{:S(2)}) copy-start(bf16[512,1024]{1,0:T(8,128)(2,1)} %param.21) | copy-start | bytes 3145732
  14.6 27.9 %all-to-all-start = ((bf16[64,32,512]{2,0,1:T(8,128)(2,1)}), bf16[64,32,512]{2,0,1:T(8,128)(2,1)S(1)}, u32[]{:S(2)}, u32[]{:S(2)}) async-start(bf16[64,32,512]{2,0,1:T(8,128)(2,1)} %multiply_convert_fusion), calls=%async_computation | async-start | bytes 4194304 | tf_op jit(solution)/shard_map/all_to_all | solution.py:89
  42.5 2.5 copy-start.7
  43.7 1.3 copy-start.5
  54.9 4.4 %copy-start.6 = (bf16[4,64,8,512]{3,2,1,0:T(8,128)(2,1)S(1)}, bf16[4,64,8,512]{3,2,1,0:T(8,128)(2,1)}, u32[]{:S(2)}) copy-start(bf16[4,64,8,512]{3,2,1,0:T(8,128)(2,1)} %copy-done.5) | copy-start | bytes 6291460
  54.9 4.4 %copy-start.8 = (bf16[512,512]{1,0:T(8,128)(2,1)S(1)}, bf16[512,512]{1,0:T(8,128)(2,1)}, u32[]{:S(2)}) copy-start(bf16[512,512]{1,0:T(8,128)(2,1)} %param.18) | copy-start | bytes 1572868
  133.0 9.4 %copy-start.3 = (bf16[64,32,512]{2,1,0:T(8,128)(2,1)S(1)}, bf16[64,32,512]{2,1,0:T(8,128)(2,1)}, u32[]{:S(2)}) copy-start(bf16[64,32,512]{2,1,0:T(8,128)(2,1)} %param.14) | copy-start | bytes 6291460
  137.7 28.8 %all-to-all-start.1 = ((bf16[256,8,512]{2,1,0:T(8,128)(2,1)}), bf16[256,8,512]{2,1,0:T(8,128)(2,1)}, u32[]{:S(2)}, u32[]{:S(2)}) async-start(bf16[256,8,512]{2,1,0:T(8,128)(2,1)} %copy.38), calls=%async_computation.1 | async-start | bytes 4194304 | tf_op jit(solution)/shard_map/all_to_all | solution.py:98
  142.2 130.2 %all-reduce.2.cloned.1.call-start = ((), (), s32[]{:S(2)}) async-start(), calls=%async_computation.2 | async-start | bytes 2097152 | tf_op jit(solution)/shard_map/psum | solution.py:119
  166.5 2.8 copy-start.4
  169.4 2.5 copy-start.9
  174.4 3.2 %copy-start.2 = (f32[2048,1024]{1,0:T(8,128)}, f32[2048,1024]{1,0:T(8,128)S(1)}, u32[]{:S(2)}) copy-start(f32[2048,1024]{1,0:T(8,128)S(1)} %get-tuple-element.231) | copy-start | bytes 25165828
  216.2 87.2 %all-gather.4.cloned.1.call-start = ((), (), s32[]{:S(2)}) async-start(), calls=%async_computation.3 | async-start | bytes 1179648 | tf_op jit(solution)/shard_map/all_gather | solution.py:146
  303.3 6.2 %copy-start.1 = (bf16[512,1024]{1,0:T(8,128)(2,1)S(1)}, bf16[512,1024]{1,0:T(8,128)(2,1)}, u32[]{:S(2)}) copy-start(bf16[512,1024]{1,0:T(8,128)(2,1)} %param.21) | copy-start | bytes 3145732
Sparse Core Ops, SparseCore 0:
  216.3 56.0 all-reduce.1
  279.3 23.9 all-gather.3
where the time goes:
time: 319 us; the launch traced here: 316 us
  waiting for transfers between devices  123 us (39%)
  matrix products  79 us (25%)
  local copies, waits for them, and re-layouts  48.1 us (15%)
  blocking collectives  29.7 us (9%)
  other arithmetic  14.3 us (4%)
  between operations  13.6 us (4%)
  starting transfers between devices  8.54 us (3%)
    psum x1, waiting for transfers between devices, local(): lax.psum(slot_partial.astype(jnp.bfloat16), 'pos').astype(jnp.float32)  56.1 us
    all_gather x2, blocking collectives, joined(): everything = jax.tree.map(lambda part: lax.all_gather(part, axis), shard)  29.7 us
    sub x8, matrix products, softmax_rows(): weights = jnp.exp(scores - largest)  25.1 us
    all_gather x1, waiting for transfers between devices, local(): lax.all_gather(outputs, 'pos', axis=0, tiled=True)  24.1 us
    all_to_all x1, waiting for transfers between devices, local(): lax.all_to_all(normed, 'frame', split_axis=1, concat_axis=0, tiled=True)  24.1 us
    dot_general x8, matrix products, one_head(): jnp.einsum('pfg,gpd->fpd', attention, values_head, preferred_element_type...  21.6 us
    unnamed x23, local copies, waits for them, and re-layouts  19.8 us
    all_to_all x1, waiting for transfers between devices, local(): lax.all_to_all(mixed_part, 'frame', split_axis=0, concat_axis=1, tiled=True)  18.5 us
  transfers between devices with their start and end apart: 4, of which 4 were waited for; matrix products, arithmetic and copies ran while one was open for 2% of the time, Pallas kernels for 0%

commit v1 on v0

--- a/solution.py
+++ b/solution.py
@@ -1,6 +1,10 @@
+import functools
+
 import jax
 import jax.numpy as jnp
 from jax import lax
+from jax.experimental import pallas as pl
+from jax.experimental.pallas import tpu as pltpu
 from jax.sharding import PartitionSpec as P
 
 HEADS = 8
@@ -39,37 +43,10 @@
     return values_in * lax.rsqrt(mean_sq + EPS) * gain
 
 
-def project(rows_in, weights):
-    return jnp.dot(rows_in, weights, preferred_element_type=jnp.float32).astype(jnp.bfloat16)
-
-
 def softmax_rows(scores, axis_index):
     largest = jnp.max(scores, axis=axis_index, keepdims=True)
     weights = jnp.exp(scores - largest)
     return (weights / jnp.sum(weights, axis=axis_index, keepdims=True)).astype(jnp.bfloat16)
-
-
-def attend(queries, keys_block, values_block):
-    frame_count = queries.shape[0]
-    score_scale = queries.shape[3] ** (-0.5)
-    causal = jnp.arange(frame_count)[:, None] >= jnp.arange(frame_count)[None, :]
-
-    def one_head(triple):
-        queries_head, keys_head, values_head = triple
-        scores = (
-            jnp.einsum("fpd,gpd->pfg", queries_head, keys_head, preferred_element_type=jnp.float32)
-            * score_scale
-        )
-        scores = jnp.where(causal[None], scores, MASKED)
-        attention = softmax_rows(scores, 2)
-        return jnp.einsum(
-            "pfg,gpd->fpd", attention, values_head, preferred_element_type=jnp.float32
-        ).astype(jnp.bfloat16)
-
-    by_head = tuple(
-        (jnp.moveaxis(array_in, 2, 0) for array_in in (queries, keys_block, values_block))
-    )
-    return jnp.moveaxis(lax.map(one_head, by_head), 0, 2)
 
 
 def merge_stats(first_pair, second_pair):
@@ -80,27 +57,8 @@
     return (largest, totals)
 
 
-def local(
-    frames_in, attn_gain, w_query, w_key, w_value, w_output, moe_gain, dispatch_keys, w_in, w_out
-):
-    frame_count, pos_count, features = frames_in.shape
-    head_dim = features // HEADS
-    normed = rms_scale(frames_in, attn_gain).astype(jnp.bfloat16)
-    spread = lax.all_to_all(normed, "frame", split_axis=1, concat_axis=0, tiled=True)
-    all_frames = spread.shape[0]
-    pos_part = spread.shape[1]
-    flattened = spread.reshape(all_frames * pos_part, features)
-    shaped = (all_frames, pos_part, HEADS, head_dim)
-    queries = project(flattened, w_query).reshape(shaped)
-    keys_block = project(flattened, w_key).reshape(shaped)
-    values_block = project(flattened, w_value).reshape(shaped)
-    mixed_part = attend(queries, keys_block, values_block).reshape(all_frames, pos_part, features)
-    mixed_heads = lax.all_to_all(mixed_part, "frame", split_axis=0, concat_axis=1, tiled=True)
-    mixed_heads = mixed_heads.reshape(frame_count * pos_count, features)
-    residual = (
-        frames_in.reshape(frame_count * pos_count, features).astype(jnp.float32)
-        + jnp.dot(mixed_heads, w_output, preferred_element_type=jnp.float32)
-    ).astype(jnp.bfloat16)
+def moe_plain(residual, moe_gain, dispatch_keys, w_in, w_out):
+    features = residual.shape[1]
     moe_input = rms_scale(residual, moe_gain).astype(jnp.bfloat16)
     logits = LOGIT_SCALE * jnp.dot(moe_input, dispatch_keys, preferred_element_type=jnp.float32)
     local_max = jnp.max(logits, axis=0)
@@ -147,7 +105,398 @@
         preferred_element_type=jnp.float32,
     )
     frames_out = (residual.astype(jnp.float32) + moe_out).astype(jnp.bfloat16)
-    return frames_out.reshape(frame_count, pos_count, features)
+    return frames_out
+
+
+MESH = pl.DeviceIdType.MESH
+NT = (((1,), (1,)), ((), ()))
+LANES = 128
+
+
+def attention_kernel(
+    count, heads, x_ref, gain_ref, wq_ref, wk_ref, wv_ref, wo_ref, out_ref,
+    normed, spread, mixed, home, in_send, in_recv, out_send, out_recv,
+):
+    me = lax.axis_index("frame")
+    steps, _, frames, features = x_ref.shape
+    rows = count * frames
+    head_dim = features // heads
+    per_group = max(1, LANES // head_dim)
+    width = per_group * head_dim
+    scale = head_dim ** (-0.5)
+
+    barrier = pltpu.get_barrier_semaphore()
+    for k in range(1, count):
+        peer = lax.rem(me + k, count)
+        pl.semaphore_signal(barrier, inc=1, device_id={"frame": peer}, device_id_type=MESH)
+    pl.semaphore_wait(barrier, count - 1)
+
+    def copy_in(i, target, source):
+        return pltpu.make_async_remote_copy(
+            src_ref=normed.at[i, target], dst_ref=spread.at[i, source],
+            send_sem=in_send.at[i, target], recv_sem=in_recv.at[i, source],
+            device_id={"frame": target}, device_id_type=MESH,
+        )
+
+    def copy_back(i, target, source):
+        return pltpu.make_async_remote_copy(
+            src_ref=mixed.at[i, target], dst_ref=home.at[i, source],
+            send_sem=out_send.at[i, target], recv_sem=out_recv.at[i, source],
+            device_id={"frame": target}, device_id_type=MESH,
+        )
+
+    def norm_step(i, carry):
+        values = x_ref[i].reshape(rows, features)
+        normed[i] = rms_scale(values, gain_ref[...]).astype(jnp.bfloat16).reshape(
+            count, frames, features
+        )
+        for k in range(1, count):
+            copy_in(i, lax.rem(me + k, count), me).start()
+        spread[i, me] = normed[i, me]
+        return carry
+
+    lax.fori_loop(0, steps, norm_step, 0)
+
+    def attend_step(i, carry):
+        for k in range(1, count):
+            peer = lax.rem(me + k, count)
+            copy_in(i, peer, peer).wait_recv()
+        tokens = spread[i].reshape(rows, features)
+        queries = jnp.dot(tokens, wq_ref[...], preferred_element_type=jnp.float32).astype(jnp.bfloat16)
+        keys = jnp.dot(tokens, wk_ref[...], preferred_element_type=jnp.float32).astype(jnp.bfloat16)
+        values = jnp.dot(tokens, wv_ref[...], preferred_element_type=jnp.float32).astype(jnp.bfloat16)
+        causal = lax.broadcasted_iota(jnp.int32, (rows, rows), 0) >= lax.broadcasted_iota(
+            jnp.int32, (rows, rows), 1
+        )
+        lane_head = lax.broadcasted_iota(jnp.int32, (1, width), 1) // head_dim
+        for group in range(features // width):
+            lanes = slice(group * width, (group + 1) * width)
+            total = jnp.zeros((rows, width), jnp.float32)
+            for j in range(per_group):
+                chosen = (lane_head == j).astype(jnp.float32)
+                scores = lax.dot_general(
+                    queries[:, lanes] * chosen.astype(jnp.bfloat16), keys[:, lanes], NT,
+                    preferred_element_type=jnp.float32,
+                ) * scale
+                scores = jnp.where(causal, scores, MASKED)
+                weights = jnp.exp(scores - jnp.max(scores, axis=1, keepdims=True))
+                sums = jnp.sum(weights, axis=1, keepdims=True)
+                part = jnp.dot(
+                    weights.astype(jnp.bfloat16), values[:, lanes], preferred_element_type=jnp.float32
+                )
+                total = total + part * (chosen / sums)
+            mixed[i, :, :, lanes] = total.astype(jnp.bfloat16).reshape(count, frames, width)
+        for k in range(1, count):
+            copy_back(i, lax.rem(me + k, count), me).start()
+        home[i, me] = mixed[i, me]
+        return carry
+
+    lax.fori_loop(0, steps, attend_step, 0)
+
+    def output_step(i, carry):
+        for k in range(1, count):
+            peer = lax.rem(me + k, count)
+            copy_back(i, peer, peer).wait_recv()
+        result = x_ref[i].reshape(rows, features).astype(jnp.float32) + jnp.dot(
+            home[i].reshape(rows, features), wo_ref[...], preferred_element_type=jnp.float32
+        )
+        out_ref[i] = result.astype(jnp.bfloat16).reshape(count, frames, features)
+        return carry
+
+    lax.fori_loop(0, steps, output_step, 0)
+
+    def drain_step(i, carry):
+        for k in range(1, count):
+            peer = lax.rem(me + k, count)
+            copy_in(i, peer, me).wait_send()
+            copy_back(i, peer, me).wait_send()
+        return carry
+
+    lax.fori_loop(0, steps, drain_step, 0)
+
+
+def attention_block(x, gain, w_query, w_key, w_value, w_output):
+    count = lax.axis_size("frame")
+    steps = x.shape[0]
+    vmem = pl.BlockSpec(memory_space=pltpu.VMEM)
+    buffer = pltpu.VMEM(x.shape, jnp.bfloat16)
+    sems = pltpu.SemaphoreType.DMA((steps, count))
+    return pl.pallas_call(
+        functools.partial(attention_kernel, count, HEADS),
+        out_shape=jax.ShapeDtypeStruct(x.shape, jnp.bfloat16),
+        in_specs=[vmem] * 6,
+        out_specs=vmem,
+        scratch_shapes=[buffer] * 4 + [sems] * 4,
+        compiler_params=pltpu.CompilerParams(
+            collective_id=0, has_side_effects=True, vmem_limit_bytes=48 * 2**20
+        ),
+    )(x, gain.reshape(1, -1), w_query, w_key, w_value, w_output)
+
+
+def moe_kernel(
+    count, res_ref, gain_ref, keys_ref, keys_t_ref, w_in_hbm, w_out_hbm, out_ref,
+    tokens, comb, part, part_stat, exch, exch_stat, merged, merged_stat, recv, recv_stat,
+    w_in, w_out, outs, total,
+    w_sem, x_send, x_recv, xs_send, xs_recv, m_send, m_recv, ms_send, ms_recv,
+    g_send, g_recv, f_send, f_recv,
+):
+    pos = lax.axis_index("pos")
+    chips = count // 2
+    chip, core = pos // 2, lax.rem(pos, 2)
+    partner = chip * 2 + 1 - core
+    rows_dev = outs.shape[1]
+    rows_chip = 2 * rows_dev
+    token_count, features = res_ref.shape
+    last = chips - 1
+
+    load_in = pltpu.make_async_copy(w_in_hbm, w_in, w_sem.at[0])
+    load_out = pltpu.make_async_copy(w_out_hbm, w_out, w_sem.at[1])
+    load_in.start()
+    load_out.start()
+
+    barrier = pltpu.get_barrier_semaphore()
+    for k in range(1, chips):
+        peer = lax.rem(chip + k, chips) * 2 + core
+        pl.semaphore_signal(barrier, inc=1, device_id={"pos": peer}, device_id_type=MESH)
+    pl.semaphore_signal(barrier, inc=1, device_id={"pos": partner}, device_id_type=MESH)
+    pl.semaphore_wait(barrier, chips)
+
+    tile = min(256, token_count)
+    tiles = token_count // tile
+
+    def tile_rows(t):
+        return pl.ds(pl.multiple_of(t * tile, tile), tile)
+
+    def norm_step(t, carry):
+        block = tile_rows(t)
+        tokens[block] = rms_scale(res_ref[block], gain_ref[...]).astype(jnp.bfloat16)
+        return carry
+
+    lax.fori_loop(0, tiles, norm_step, 0)
+
+    eye = lax.broadcasted_iota(jnp.int32, (rows_dev, rows_dev), 0) == lax.broadcasted_iota(
+        jnp.int32, (rows_dev, rows_dev), 1
+    )
+
+    def as_row(column):
+        return jnp.sum(jnp.where(eye, column, 0.0), axis=0, keepdims=True)
+
+    def as_column(row):
+        return jnp.sum(jnp.where(eye, row, 0.0), axis=1, keepdims=True)
+
+    def pair(src, dst, sends, recvs, k, target):
+        return pltpu.make_async_remote_copy(
+            src_ref=src, dst_ref=dst, send_sem=sends.at[k], recv_sem=recvs.at[k],
+            device_id={"pos": target}, device_id_type=MESH,
+        )
+
+    def exchange(k):
+        return (
+            pair(part.at[k, 1 - core], exch.at[k], x_send, x_recv, k, partner),
+            pair(part_stat.at[k, 1 - core], exch_stat.at[k], xs_send, xs_recv, k, partner),
+        )
+
+    def scatter(k):
+        target = lax.rem(chip + last - k, chips) * 2 + core
+        return (
+            pair(merged.at[k], recv.at[k], m_send, m_recv, k, target),
+            pair(merged_stat.at[k], recv_stat.at[k], ms_send, ms_recv, k, target),
+        )
+
+    def dispatch(k):
+        target = lax.rem(chip + last - k, chips)
+        chunk = keys_t_ref[pl.ds(pl.multiple_of(target * rows_chip, rows_chip), rows_chip)]
+        logits = LOGIT_SCALE * lax.dot_general(
+            chunk, tokens[...], NT, preferred_element_type=jnp.float32
+        )
+        largest = jnp.max(logits, axis=1, keepdims=True)
+        weights = jnp.exp(logits - largest)
+        sums = jnp.sum(weights, axis=1, keepdims=True)
+        sent = jnp.dot(
+            weights.astype(jnp.bfloat16), tokens[...], preferred_element_type=jnp.float32
+        ).astype(jnp.bfloat16)
+        for c in range(2):
+            own = slice(c * rows_dev, (c + 1) * rows_dev)
+            part[k, c] = sent[own]
+            part_stat[k, c, 0:1, :] = as_row(largest[own])
+            part_stat[k, c, 1:2, :] = as_row(sums[own])
+        for copy in exchange(k):
+            copy.start()
+
+    def merge_pair(k):
+        for copy in exchange(k):
+            copy.wait_recv()
+        mine, other = part_stat[k, core], exch_stat[k]
+        largest = jnp.maximum(mine[0:1], other[0:1])
+        scale_mine = jnp.exp(mine[0:1] - largest)
+        scale_other = jnp.exp(other[0:1] - largest)
+        merged_stat[k, 0:1, :] = largest
+        merged_stat[k, 1:2, :] = mine[1:2] * scale_mine + other[1:2] * scale_other
+        merged[k] = (
+            part[k, core].astype(jnp.float32) * as_column(scale_mine)
+            + exch[k].astype(jnp.float32) * as_column(scale_other)
+        ).astype(jnp.bfloat16)
+
+    part_stat[...] = jnp.zeros_like(part_stat)
+    merged_stat[...] = jnp.zeros_like(merged_stat)
+
+    def dispatch_step(k, carry):
+        dispatch(k)
+
+        @pl.when(k >= 1)
+        def _():
+            merge_pair(k - 1)
+            for copy in scatter(k - 1):
+                copy.start()
+
+        return carry
+
+    lax.fori_loop(0, chips, dispatch_step, 0)
+
+    def combine_step(t, carry):
+        block = tile_rows(t)
+        logits = LOGIT_SCALE * jnp.dot(
+            tokens[block], keys_ref[...], preferred_element_type=jnp.float32
+        )
+        weights = jnp.exp(logits - jnp.max(logits, axis=1, keepdims=True))
+        weights = (weights / jnp.sum(weights, axis=1, keepdims=True)).astype(jnp.bfloat16)
+        for c in range(chips):
+            comb[c, block] = weights[:, c * rows_chip : (c + 1) * rows_chip]
+        return carry
+
+    lax.fori_loop(0, tiles, combine_step, 0)
+
+    merge_pair(last)
+    for k in range(last):
+        for copy in scatter(k):
+            copy.wait_recv()
+    stats = [recv_stat[k] for k in range(last)] + [merged_stat[last]]
+    blocks = [recv[k] for k in range(last)] + [merged[last]]
+    largest = functools.reduce(jnp.maximum, [stat[0:1] for stat in stats])
+    scales = [jnp.exp(stat[0:1] - largest) for stat in stats]
+    sums = sum(stat[1:2] * scale for stat, scale in zip(stats, scales))
+    slot_in = sum(
+        block.astype(jnp.float32) * as_column(scale / sums) for block, scale in zip(blocks, scales)
+    ).astype(jnp.bfloat16)
+
+    load_in.wait()
+    load_out.wait()
+    for e in range(w_in.shape[0]):
+        own = slice(e * SLOTS, (e + 1) * SLOTS)
+        hidden = jax.nn.gelu(
+            jnp.dot(slot_in[own], w_in[e], preferred_element_type=jnp.float32)
+        ).astype(jnp.bfloat16)
+        outs[pos, own] = jnp.dot(hidden, w_out[e], preferred_element_type=jnp.float32).astype(
+            jnp.bfloat16
+        )
+
+    def gather(k, target, source):
+        return pair(outs.at[source], outs.at[source], g_send, g_recv, k, target)
+
+    def forward(k, source):
+        return pair(outs.at[source], outs.at[source], f_send, f_recv, k, partner)
+
+    def chip_at(k):
+        return lax.rem(chip + chips - k, chips)
+
+    for k in range(1, chips):
+        gather(k, lax.rem(chip + k, chips) * 2 + core, pos).start()
+    forward(0, pos).start()
+
+    def add_chip(k, source, first, final):
+        pair_rows = outs[pl.ds(source * 2, 2)].reshape(rows_chip, features)
+
+        def add_step(t, carry):
+            block = tile_rows(t)
+            before = res_ref[block].astype(jnp.float32) if first else total[block]
+            result = before + jnp.dot(
+                comb[source, block], pair_rows, preferred_element_type=jnp.float32
+            )
+            if final:
+                out_ref[block] = result.astype(jnp.bfloat16)
+            else:
+                total[block] = result
+            return carry
+
+        lax.fori_loop(0, tiles, add_step, 0)
+
+    order = sorted(range(1, chips), key=lambda k: min(k, chips - k))
+    forward(0, partner).wait_recv()
+    waiting = 0
+    for step, k in enumerate(order + [None]):
+        if k is not None:
+            source = chip_at(k) * 2 + core
+            gather(k, pos, source).wait_recv()
+            forward(k, source).start()
+        add_chip(waiting, chip_at(waiting), step == 0, k is None)
+        if k is not None:
+            forward(k, chip_at(k) * 2 + 1 - core).wait_recv()
+            waiting = k
+
+    for k in range(chips):
+        for copy in exchange(k):
+            copy.wait_send()
+        forward(k, pos).wait_send()
+    for k in range(last):
+        for copy in scatter(k):
+            copy.wait_send()
+        gather(k + 1, pos, pos).wait_send()
+
+
+def moe_block(residual, gain, dispatch_keys, w_in, w_out):
+    count = lax.axis_size("pos")
+    chips = count // 2
+    token_count, features = residual.shape
+    slots = dispatch_keys.shape[1]
+    rows_dev = slots // count
+    vmem = pl.BlockSpec(memory_space=pltpu.VMEM)
+    anywhere = pl.BlockSpec(memory_space=pl.ANY)
+    half = jnp.bfloat16
+
+    def rows(*lead):
+        return pltpu.VMEM(lead + (rows_dev, features), half)
+
+    def stat(*lead):
+        return pltpu.VMEM(lead + (8, rows_dev), jnp.float32)
+
+    sems = pltpu.SemaphoreType.DMA((chips,))
+    return pl.pallas_call(
+        functools.partial(moe_kernel, count),
+        out_shape=jax.ShapeDtypeStruct(residual.shape, half),
+        in_specs=[vmem] * 4 + [anywhere] * 2,
+        out_specs=vmem,
+        scratch_shapes=[
+            pltpu.VMEM((token_count, features), half),
+            pltpu.VMEM((chips, token_count, 2 * rows_dev), half),
+            rows(chips, 2), stat(chips, 2), rows(chips), stat(chips),
+            rows(chips), stat(chips), rows(chips), stat(chips),
+            pltpu.VMEM(w_in.shape, half), pltpu.VMEM(w_out.shape, half),
+            rows(count), pltpu.VMEM((token_count, features), jnp.float32),
+            pltpu.SemaphoreType.DMA((2,)),
+        ] + [sems] * 12,
+        compiler_params=pltpu.CompilerParams(
+            collective_id=1, has_side_effects=True, vmem_limit_bytes=56 * 2**20
+        ),
+    )(residual, gain.reshape(1, -1), dispatch_keys, dispatch_keys.T, w_in, w_out)
+
+
+def local(
+    frames_in, attn_gain, w_query, w_key, w_value, w_output, moe_gain, dispatch_keys, w_in, w_out
+):
+    frame_count, pos_count, features = frames_in.shape
+    blocks = lax.axis_size("frame")
+    steps = pos_count // blocks
+    x = frames_in.reshape(frame_count, blocks, steps, features).transpose(2, 1, 0, 3)
+    residual = attention_block(x, attn_gain, w_query, w_key, w_value, w_output)
+    residual = residual.reshape(frame_count * pos_count, features)
+    count_pos = lax.axis_size("pos")
+    whole_experts = w_in.shape[0] * count_pos == EXPERTS and count_pos % 2 == 0
+    if whole_experts and dispatch_keys.shape[1] // count_pos % LANES == 0:
+        frames_out = moe_block(residual, moe_gain, dispatch_keys, w_in, w_out)
+    else:
+        frames_out = moe_plain(residual, moe_gain, dispatch_keys, w_in, w_out)
+    frames_out = frames_out.reshape(steps, blocks, frame_count, features)
+    return frames_out.transpose(2, 1, 0, 3).reshape(frame_count, pos_count, features)
 
 
 def solution(mesh):

time: 319 us -> 106 us (0.33)
  waiting for transfers between devices: 123 us -> 0 us
  Pallas kernels: 0 us -> 95.8 us
  matrix products: 79 us -> 0 us
  local copies, waits for them, and re-layouts: 48.1 us -> 10.3 us
  blocking collectives: 29.7 us -> 0 us
  other arithmetic: 14.3 us -> 0 us
  between operations: 13.6 us -> 0.07 us
  starting transfers between devices: 8.54 us -> 0 us
    pallas_call x0 -> x2, Pallas kernels: none -> 95.8 us  [the longest x1 51.5 us: attention_block(): pl.pallas_call(functools.partial(attention_kernel, count, HEADS), out_sha...]
    psum x1 -> x0, waiting for transfers between devices: 56.1 us -> none  [local(): lax.psum(slot_partial.astype(jnp.bfloat16), 'pos').astype(jnp.float32)]
    dot_general x16 -> x0, matrix products: 53.8 us -> none  [the longest x8 21.6 us: one_head(): jnp.einsum('pfg,gpd->fpd', attention, values_head, preferred_element_type...]
    all_to_all x2 -> x0, waiting for transfers between devices: 42.6 us -> none  [the longest x1 24.1 us: local(): lax.all_to_all(normed, 'frame', split_axis=1, concat_axis=0, tiled=True)]
    all_gather x2 -> x0, blocking collectives: 29.7 us -> none  [joined(): everything = jax.tree.map(lambda part: lax.all_gather(part, axis), shard)]
    sub x8 -> x0, matrix products: 25.1 us -> none  [softmax_rows(): weights = jnp.exp(scores - largest)]
    all_gather x1 -> x0, waiting for transfers between devices: 24.1 us -> none  [local(): lax.all_gather(outputs, 'pos', axis=0, tiled=True)]
    reshape x4 -> x1, local copies, waits for them, and re-layouts: 20.7 us -> 2.48 us  [local(): frames_in.reshape(frame_count, blocks, steps, features)]
  transfers between devices with their start and end apart: 4 -> 0, of which waited for: 4 -> 0; matrix products, arithmetic and copies ran while one was open for 2% -> 0% of each run, Pallas kernels for 0% -> 0%
where the time goes in v1:
time: 106 us
  Pallas kernels  95.8 us (90%)
  local copies, waits for them, and re-layouts  10.3 us (10%)
    pallas_call x1, Pallas kernels, attention_block(): pl.pallas_call(functools.partial(attention_kernel, count, HEADS), out_sha...  51.5 us
    pallas_call x1, Pallas kernels, moe_block(): pl.pallas_call(functools.partial(moe_kernel, count), out_shape=jax.ShapeD...  44.3 us
    transpose x1, local copies, waits for them, and re-layouts, local(): frames_out.transpose(2, 1, 0, 3).reshape(frame_count, pos_count, features)  4.07 us
    unnamed x15, local copies, waits for them, and re-layouts  3.78 us
    reshape x1, local copies, waits for them, and re-layouts, local(): frames_in.reshape(frame_count, blocks, steps, features)  2.48 us

profile of v1, /device:TPU:9, one launch (start us, length us, event | category | flops | bytes accessed | tf_op | source)
XLA Modules:
  0.0 106.2 jit_solution(11437416606471966629)
XLA Ops:
  0.0 0.0 copy-start.6
  0.0 2.4 %copy.14 = bf16[512,1024]{0,1:T(8,128)(2,1)} copy(bf16[512,1024]{1,0:T(8,128)(2,1)} %keys_ref.1) | data formatting | bytes 2097152 | tf_op args[7]
  2.4 0.0 copy-done.6
  2.4 0.0 copy-start.1
  2.4 0.0 copy-start.2
  2.5 0.0 copy-start.3
  2.5 0.0 copy-start.4
  2.5 0.0 copy-start.5
  2.5 2.5 %copy.19 = bf16[64,4,8,512]{3,0,1,2:T(8,128)(2,1)} copy(bf16[64,4,8,512]{3,2,1,0:T(8,128)(2,1)S(1)} %bitcast.19) | data formatting | bytes 4194304 | tf_op jit(solution)/shard_map/reshape | solution.py:489
  5.0 0.0 copy-done.1
  5.0 0.0 copy-done.2
  5.0 0.0 copy-done.3
  5.0 0.0 copy-done.4
  5.0 0.0 copy-done.5
  5.0 51.5 %shard_map.100 = bf16[8,4,64,512]{3,2,1,0:T(8,128)(2,1)S(1)} custom-call(bf16[8,4,64,512]{3,2,1,0:T(8,128)(2,1)} %bitcast.16, f32[1,512]{1,0:T(1,128)S(1)} %bitcast.15, bf16[512,512]{1,0:T(8,128)(2,1)S(1)} %copy-done.1, bf16[512,512]{1,0:T(8,128)(2,1)S(1)} %copy-done.2, bf16[512,512]{1,0:T(8,128)(2,1)S(1)} %copy-done.3, bf16[512,512]{1,0:T(8,128)(2,1)S(1)} %copy-done.4), custom_call_target="tpu_custom_call" | custom-call | tf_op jit(solution)/shard_map/pallas_call | solution.py:224
  56.5 0.0 copy-start
  56.5 1.3 %copy-done = bf16[8,4,64,512]{3,2,1,0:T(8,128)(2,1)} copy-done((bf16[8,4,64,512]{3,2,1,0:T(8,128)(2,1)}, bf16[8,4,64,512]{3,2,1,0:T(8,128)(2,1)S(1)}, u32[]{:S(2)}) %copy-start) | copy-done | bytes 2097176
  57.8 44.3 %shard_map.101 = bf16[2048,512]{1,0:T(8,128)(2,1)} custom-call(bf16[2048,512]{1,0:T(8,128)(2,1)} %bitcast.14, f32[1,512]{1,0:T(1,128)} %bitcast.20, bf16[512,1024]{1,0:T(8,128)(2,1)} %keys_ref.1, bf16[1024,512]{1,0:T(8,128)(2,1)} %bitcast.18, bf16[2,512,2048]{2,1,0:T(8,128)(2,1)} %w_in_hbm.1, bf16[2,2048,512]{2,1,0:T(8,128)(2,1)} %w_out_hbm.1), custom_call_target="tpu_custom_call" | custom-call | tf_op jit(solution)/shard_map/pallas_call | solution.py:463
  102.1 4.1 %copy.18 = bf16[64,4,8,512]{3,2,1,0:T(8,128)(2,1)} copy(bf16[64,4,8,512]{3,0,1,2:T(8,128)(2,1)} %bitcast.17) | data formatting | bytes 4194304 | tf_op jit(solution)/shard_map/transpose | solution.py:499
Async XLA Ops:
  0.0 2.4 %copy-start.6 = (bf16[64,32,512]{2,1,0:T(8,128)(2,1)S(1)}, bf16[64,32,512]{2,1,0:T(8,128)(2,1)}, u32[]{:S(2)}) copy-start(bf16[64,32,512]{2,1,0:T(8,128)(2,1)} %param.10) | copy-start | bytes 6291460
  2.4 2.5 %copy-start.1 = (bf16[512,512]{1,0:T(8,128)(2,1)S(1)}, bf16[512,512]{1,0:T(8,128)(2,1)}, u32[]{:S(2)}) copy-start(bf16[512,512]{1,0:T(8,128)(2,1)} %wq_ref.1) | copy-start | bytes 1572868
  2.4 2.5 %copy-start.2 = (bf16[512,512]{1,0:T(8,128)(2,1)S(1)}, bf16[512,512]{1,0:T(8,128)(2,1)}, u32[]{:S(2)}) copy-start(bf16[512,512]{1,0:T(8,128)(2,1)} %wk_ref.1) | copy-start | bytes 1572868
  2.5 2.5 %copy-start.3 = (bf16[512,512]{1,0:T(8,128)(2,1)S(1)}, bf16[512,512]{1,0:T(8,128)(2,1)}, u32[]{:S(2)}) copy-start(bf16[512,512]{1,0:T(8,128)(2,1)} %wv_ref.1) | copy-start | bytes 1572868
  2.5 2.5 %copy-start.4 = (bf16[512,512]{1,0:T(8,128)(2,1)S(1)}, bf16[512,512]{1,0:T(8,128)(2,1)}, u32[]{:S(2)}) copy-start(bf16[512,512]{1,0:T(8,128)(2,1)} %wo_ref.1) | copy-start | bytes 1572868
  2.5 2.5 %copy-start.5 = (f32[512]{0:T(512)S(1)}, f32[512]{0:T(512)}, u32[]{:S(2)}) copy-start(f32[512]{0:T(512)} %param.11) | copy-start | bytes 6148
  56.5 1.3 %copy-start = (bf16[8,4,64,512]{3,2,1,0:T(8,128)(2,1)}, bf16[8,4,64,512]{3,2,1,0:T(8,128)(2,1)S(1)}, u32[]{:S(2)}) copy-start(bf16[8,4,64,512]{3,2,1,0:T(8,128)(2,1)S(1)} %shard_map.100) | copy-start | bytes 6291460

commit v2 on v1

--- a/solution.py
+++ b/solution.py
@@ -113,8 +113,21 @@
 LANES = 128
 
 
-def attention_kernel(
-    count, heads, x_ref, gain_ref, wq_ref, wk_ref, wv_ref, wo_ref, out_ref,
+def greet(peers):
+    barrier = pltpu.get_barrier_semaphore()
+    for peer in peers:
+        pl.semaphore_signal(barrier, inc=1, device_id=peer, device_id_type=MESH)
+    pl.semaphore_wait(barrier, len(peers))
+
+
+def frame_peers(count):
+    me = lax.axis_index("frame")
+    return [{"frame": lax.rem(me + k, count)} for k in range(1, count)]
+
+
+def attention_phases(
+    count, heads, load_x, load_weights, emit_tile,
+    x_ref, gain_ref, wq_ref, wk_ref, wv_ref, wo_ref,
     normed, spread, mixed, home, in_send, in_recv, out_send, out_recv,
 ):
     me = lax.axis_index("frame")
@@ -125,12 +138,6 @@
     width = per_group * head_dim
     scale = head_dim ** (-0.5)
 
-    barrier = pltpu.get_barrier_semaphore()
-    for k in range(1, count):
-        peer = lax.rem(me + k, count)
-        pl.semaphore_signal(barrier, inc=1, device_id={"frame": peer}, device_id_type=MESH)
-    pl.semaphore_wait(barrier, count - 1)
-
     def copy_in(i, target, source):
         return pltpu.make_async_remote_copy(
             src_ref=normed.at[i, target], dst_ref=spread.at[i, source],
@@ -146,6 +153,7 @@
         )
 
     def norm_step(i, carry):
+        load_x(i)
         values = x_ref[i].reshape(rows, features)
         normed[i] = rms_scale(values, gain_ref[...]).astype(jnp.bfloat16).reshape(
             count, frames, features
@@ -156,6 +164,7 @@
         return carry
 
     lax.fori_loop(0, steps, norm_step, 0)
+    load_weights()
 
     def attend_step(i, carry):
         for k in range(1, count):
@@ -200,7 +209,7 @@
         result = x_ref[i].reshape(rows, features).astype(jnp.float32) + jnp.dot(
             home[i].reshape(rows, features), wo_ref[...], preferred_element_type=jnp.float32
         )
-        out_ref[i] = result.astype(jnp.bfloat16).reshape(count, frames, features)
+        emit_tile(i, result.astype(jnp.bfloat16))
         return carry
 
     lax.fori_loop(0, steps, output_step, 0)
@@ -212,7 +221,21 @@
             copy_back(i, peer, me).wait_send()
         return carry
 
-    lax.fori_loop(0, steps, drain_step, 0)
+    return lambda: lax.fori_loop(0, steps, drain_step, 0)
+
+
+def attention_kernel(
+    count, heads, x_ref, gain_ref, wq_ref, wk_ref, wv_ref, wo_ref, out_ref, *scratch
+):
+    greet(frame_peers(count))
+
+    def emit_tile(i, result):
+        out_ref[i] = result.reshape(out_ref.shape[1:])
+
+    attention_phases(
+        count, heads, lambda i: None, lambda: None, emit_tile,
+        x_ref, gain_ref, wq_ref, wk_ref, wv_ref, wo_ref, *scratch,
+    )()
 
 
 def attention_block(x, gain, w_query, w_key, w_value, w_output):
@@ -228,18 +251,24 @@
         out_specs=vmem,
         scratch_shapes=[buffer] * 4 + [sems] * 4,
         compiler_params=pltpu.CompilerParams(
-            collective_id=0, has_side_effects=True, vmem_limit_bytes=48 * 2**20
+            collective_id=1, has_side_effects=True, vmem_limit_bytes=48 * 2**20
         ),
     )(x, gain.reshape(1, -1), w_query, w_key, w_value, w_output)
 
 
-def moe_kernel(
-    count, res_ref, gain_ref, keys_ref, keys_t_ref, w_in_hbm, w_out_hbm, out_ref,
-    tokens, comb, part, part_stat, exch, exch_stat, merged, merged_stat, recv, recv_stat,
-    w_in, w_out, outs, total,
-    w_sem, x_send, x_recv, xs_send, xs_recv, m_send, m_recv, ms_send, ms_recv,
+def layer_kernel(
+    frames, count, heads,
+    x_hbm, gain_ref, moe_gain_ref, wq_hbm, wk_hbm, wv_hbm, wo_hbm, keys_hbm, w_in_hbm, w_out_hbm,
+    out_ref,
+    x_ref, wq, wk, wv, wo, keys_ref, w_in, w_out, x_sem, w_sem,
+    normed, spread, mixed, home, in_send, in_recv, out_send, out_recv,
+    keys_t, res_ref, tokens, comb, slot_sum, slot_max, slot_total,
+    part, part_stat, exch, exch_stat, merged, merged_stat, recv, recv_stat,
+    outs, total,
+    x_send, x_recv, xs_send, xs_recv, m_send, m_recv, ms_send, ms_recv,
     g_send, g_recv, f_send, f_recv,
 ):
+    steps = x_ref.shape[0]
     pos = lax.axis_index("pos")
     chips = count // 2
     chip, core = pos // 2, lax.rem(pos, 2)
@@ -248,31 +277,47 @@
     rows_chip = 2 * rows_dev
     token_count, features = res_ref.shape
     last = chips - 1
-
-    load_in = pltpu.make_async_copy(w_in_hbm, w_in, w_sem.at[0])
-    load_out = pltpu.make_async_copy(w_out_hbm, w_out, w_sem.at[1])
-    load_in.start()
-    load_out.start()
-
-    barrier = pltpu.get_barrier_semaphore()
-    for k in range(1, chips):
-        peer = lax.rem(chip + k, chips) * 2 + core
-        pl.semaphore_signal(barrier, inc=1, device_id={"pos": peer}, device_id_type=MESH)
-    pl.semaphore_signal(barrier, inc=1, device_id={"pos": partner}, device_id_type=MESH)
-    pl.semaphore_wait(barrier, chips)
-
-    tile = min(256, token_count)
-    tiles = token_count // tile
+    tiles = steps
+    tile = token_count // tiles
+
+    def load_step(i, carry):
+        pltpu.make_async_copy(x_hbm.at[i], x_ref.at[i], x_sem.at[i]).start()
+        return carry
+
+    lax.fori_loop(0, steps, load_step, 0)
+    early = [
+        pltpu.make_async_copy(src, dst, w_sem.at[n])
+        for n, (src, dst) in enumerate(
+            ((wq_hbm, wq), (wk_hbm, wk), (wv_hbm, wv), (wo_hbm, wo), (keys_hbm, keys_ref))
+        )
+    ]
+    late = [
+        pltpu.make_async_copy(src, dst, w_sem.at[len(early) + n])
+        for n, (src, dst) in enumerate(((w_in_hbm, w_in), (w_out_hbm, w_out)))
+    ]
+    for copy in early:
+        copy.start()
+
+    greet(
+        frame_peers(frames)
+        + [{"pos": lax.rem(chip + k, chips) * 2 + core} for k in range(1, chips)]
+        + [{"pos": partner}]
+    )
+
+    def load_x(i):
+        pltpu.make_async_copy(x_hbm.at[i], x_ref.at[i], x_sem.at[i]).wait()
+
+    def load_weights():
+        for copy in late:
+            copy.start()
+        for copy in early:
+            copy.wait()
+        for c in range(keys_t.shape[0] // LANES):
+            own = slice(c * LANES, (c + 1) * LANES)
+            keys_t[own] = keys_ref[:, own].T
 
     def tile_rows(t):
         return pl.ds(pl.multiple_of(t * tile, tile), tile)
-
-    def norm_step(t, carry):
-        block = tile_rows(t)
-        tokens[block] = rms_scale(res_ref[block], gain_ref[...]).astype(jnp.bfloat16)
-        return carry
-
-    lax.fori_loop(0, tiles, norm_step, 0)
 
     eye = lax.broadcasted_iota(jnp.int32, (rows_dev, rows_dev), 0) == lax.broadcasted_iota(
         jnp.int32, (rows_dev, rows_dev), 1
@@ -303,18 +348,61 @@
             pair(merged_stat.at[k], recv_stat.at[k], ms_send, ms_recv, k, target),
         )
 
+    part_stat[...] = jnp.zeros_like(part_stat)
+    merged_stat[...] = jnp.zeros_like(merged_stat)
+    slot_sum[...] = jnp.zeros_like(slot_sum)
+    slot_total[...] = jnp.zeros_like(slot_total)
+    slot_max[...] = jnp.full_like(slot_max, MASKED)
+
+    def add_tile(t, c):
+        block = tokens[tile_rows(t)]
+        logits = LOGIT_SCALE * lax.dot_general(
+            keys_t[pl.ds(pl.multiple_of(c * rows_chip, rows_chip), rows_chip)], block, NT,
+            preferred_element_type=jnp.float32,
+        )
+        before = slot_max[c]
+        largest = jnp.maximum(before, jnp.max(logits, axis=1, keepdims=True))
+        weights = jnp.exp(logits - largest)
+        fade = jnp.exp(before - largest)
+        sums = slot_total[c] * fade + jnp.sum(weights, axis=1, keepdims=True)
+        summed = slot_sum[c] * fade + jnp.dot(
+            weights.astype(jnp.bfloat16), block, preferred_element_type=jnp.float32
+        )
+        return largest, sums, summed
+
+    def combine_tile(t):
+        block = tile_rows(t)
+        logits = LOGIT_SCALE * jnp.dot(
+            tokens[block], keys_ref[...], preferred_element_type=jnp.float32
+        )
+        weights = jnp.exp(logits - jnp.max(logits, axis=1, keepdims=True))
+        weights = (weights / jnp.sum(weights, axis=1, keepdims=True)).astype(jnp.bfloat16)
+        for c in range(chips):
+            comb[c, block] = weights[:, c * rows_chip : (c + 1) * rows_chip]
+
+    def emit_tile(t, result):
+        block = tile_rows(t)
+        res_ref[block] = result
+        tokens[block] = rms_scale(result, moe_gain_ref[...]).astype(jnp.bfloat16)
+
+        @pl.when(t < tiles - 1)
+        def _():
+            def chunk_step(c, carry):
+                slot_max[c], slot_total[c], slot_sum[c] = add_tile(t, c)
+                return carry
+
+            lax.fori_loop(0, chips, chunk_step, 0)
+            combine_tile(t)
+
+    drain = attention_phases(
+        frames, heads, load_x, load_weights, emit_tile,
+        x_ref, gain_ref, wq, wk, wv, wo,
+        normed, spread, mixed, home, in_send, in_recv, out_send, out_recv,
+    )
+
     def dispatch(k):
-        target = lax.rem(chip + last - k, chips)
-        chunk = keys_t_ref[pl.ds(pl.multiple_of(target * rows_chip, rows_chip), rows_chip)]
-        logits = LOGIT_SCALE * lax.dot_general(
-            chunk, tokens[...], NT, preferred_element_type=jnp.float32
-        )
-        largest = jnp.max(logits, axis=1, keepdims=True)
-        weights = jnp.exp(logits - largest)
-        sums = jnp.sum(weights, axis=1, keepdims=True)
-        sent = jnp.dot(
-            weights.astype(jnp.bfloat16), tokens[...], preferred_element_type=jnp.float32
-        ).astype(jnp.bfloat16)
+        largest, sums, summed = add_tile(tiles - 1, lax.rem(chip + last - k, chips))
+        sent = summed.astype(jnp.bfloat16)
         for c in range(2):
             own = slice(c * rows_dev, (c + 1) * rows_dev)
             part[k, c] = sent[own]
@@ -337,9 +425,6 @@
             + exch[k].astype(jnp.float32) * as_column(scale_other)
         ).astype(jnp.bfloat16)
 
-    part_stat[...] = jnp.zeros_like(part_stat)
-    merged_stat[...] = jnp.zeros_like(merged_stat)
-
     def dispatch_step(k, carry):
         dispatch(k)
 
@@ -353,20 +438,8 @@
 
     lax.fori_loop(0, chips, dispatch_step, 0)
 
-    def combine_step(t, carry):
-        block = tile_rows(t)
-        logits = LOGIT_SCALE * jnp.dot(
-            tokens[block], keys_ref[...], preferred_element_type=jnp.float32
-        )
-        weights = jnp.exp(logits - jnp.max(logits, axis=1, keepdims=True))
-        weights = (weights / jnp.sum(weights, axis=1, keepdims=True)).astype(jnp.bfloat16)
-        for c in range(chips):
-            comb[c, block] = weights[:, c * rows_chip : (c + 1) * rows_chip]
-        return carry
-
-    lax.fori_loop(0, tiles, combine_step, 0)
-
     merge_pair(last)
+    combine_tile(tiles - 1)
     for k in range(last):
         for copy in scatter(k):
             copy.wait_recv()
@@ -379,8 +452,8 @@
         block.astype(jnp.float32) * as_column(scale / sums) for block, scale in zip(blocks, scales)
     ).astype(jnp.bfloat16)
 
-    load_in.wait()
-    load_out.wait()
+    for copy in late:
+        copy.wait()
     for e in range(w_in.shape[0]):
         own = slice(e * SLOTS, (e + 1) * SLOTS)
         hidden = jax.nn.gelu(
@@ -433,6 +506,7 @@
             forward(k, chip_at(k) * 2 + 1 - core).wait_recv()
             waiting = k
 
+    drain()
     for k in range(chips):
         for copy in exchange(k):
             copy.wait_send()
@@ -443,10 +517,13 @@
         gather(k + 1, pos, pos).wait_send()
 
 
-def moe_block(residual, gain, dispatch_keys, w_in, w_out):
-    count = lax.axis_size("pos")
+def layer_block(
+    x, attn_gain, moe_gain, w_query, w_key, w_value, w_output, dispatch_keys, w_in, w_out
+):
+    frames, count = lax.axis_size("frame"), lax.axis_size("pos")
     chips = count // 2
-    token_count, features = residual.shape
+    steps, features = x.shape[0], x.shape[-1]
+    token_count = x.size // features
     slots = dispatch_keys.shape[1]
     rows_dev = slots // count
     vmem = pl.BlockSpec(memory_space=pltpu.VMEM)
@@ -459,25 +536,35 @@
     def stat(*lead):
         return pltpu.VMEM(lead + (8, rows_dev), jnp.float32)
 
+    def like(array):
+        return pltpu.VMEM(array.shape, half)
+
     sems = pltpu.SemaphoreType.DMA((chips,))
+    step_sems = pltpu.SemaphoreType.DMA((steps, frames))
+    column = pltpu.VMEM((chips, 2 * rows_dev, 1), jnp.float32)
+    weights = (w_query, w_key, w_value, w_output, dispatch_keys, w_in, w_out)
     return pl.pallas_call(
-        functools.partial(moe_kernel, count),
-        out_shape=jax.ShapeDtypeStruct(residual.shape, half),
-        in_specs=[vmem] * 4 + [anywhere] * 2,
+        functools.partial(layer_kernel, frames, count, HEADS),
+        out_shape=jax.ShapeDtypeStruct((token_count, features), half),
+        in_specs=[anywhere] + [vmem] * 2 + [anywhere] * len(weights),
         out_specs=vmem,
-        scratch_shapes=[
+        scratch_shapes=[like(x)] + [like(weight) for weight in weights]
+        + [pltpu.SemaphoreType.DMA((steps,)), pltpu.SemaphoreType.DMA((len(weights),))]
+        + [like(x)] * 4 + [step_sems] * 4
+        + [
+            pltpu.VMEM((slots, features), half),
+            pltpu.VMEM((token_count, features), half),
             pltpu.VMEM((token_count, features), half),
             pltpu.VMEM((chips, token_count, 2 * rows_dev), half),
+            pltpu.VMEM((chips, 2 * rows_dev, features), jnp.float32), column, column,
             rows(chips, 2), stat(chips, 2), rows(chips), stat(chips),
             rows(chips), stat(chips), rows(chips), stat(chips),
-            pltpu.VMEM(w_in.shape, half), pltpu.VMEM(w_out.shape, half),
             rows(count), pltpu.VMEM((token_count, features), jnp.float32),
-            pltpu.SemaphoreType.DMA((2,)),
         ] + [sems] * 12,
         compiler_params=pltpu.CompilerParams(
-            collective_id=1, has_side_effects=True, vmem_limit_bytes=56 * 2**20
+            collective_id=0, has_side_effects=True, vmem_limit_bytes=60 * 2**20
         ),
-    )(residual, gain.reshape(1, -1), dispatch_keys, dispatch_keys.T, w_in, w_out)
+    )(x, attn_gain.reshape(1, -1), moe_gain.reshape(1, -1), *weights)
 
 
 def local(
@@ -487,13 +574,15 @@
     blocks = lax.axis_size("frame")
     steps = pos_count // blocks
     x = frames_in.reshape(frame_count, blocks, steps, features).transpose(2, 1, 0, 3)
-    residual = attention_block(x, attn_gain, w_query, w_key, w_value, w_output)
-    residual = residual.reshape(frame_count * pos_count, features)
     count_pos = lax.axis_size("pos")
     whole_experts = w_in.shape[0] * count_pos == EXPERTS and count_pos % 2 == 0
     if whole_experts and dispatch_keys.shape[1] // count_pos % LANES == 0:
-        frames_out = moe_block(residual, moe_gain, dispatch_keys, w_in, w_out)
+        frames_out = layer_block(
+            x, attn_gain, moe_gain, w_query, w_key, w_value, w_output, dispatch_keys, w_in, w_out
+        )
     else:
+        residual = attention_block(x, attn_gain, w_query, w_key, w_value, w_output)
+        residual = residual.reshape(frame_count * pos_count, features)
         frames_out = moe_plain(residual, moe_gain, dispatch_keys, w_in, w_out)
     frames_out = frames_out.reshape(steps, blocks, frame_count, features)
     return frames_out.transpose(2, 1, 0, 3).reshape(frame_count, pos_count, features)

time: 106 us -> 108 us (1.019)
  Pallas kernels: 95.8 us -> 100 us
  local copies, waits for them, and re-layouts: 10.3 us -> 8.14 us
    pallas_call x2 -> x1, Pallas kernels: 95.8 us -> 100 us  [layer_block(): pl.pallas_call(functools.partial(layer_kernel, frames, count, HEADS), out...]
    unnamed x15 -> x0, local copies, waits for them, and re-layouts: 3.78 us -> none
    reshape x1, local copies, waits for them, and re-layouts: 2.48 us -> 4.07 us  [local(): frames_in.reshape(frame_count, blocks, steps, features)]
where the time goes in v2:
time: 108 us
  Pallas kernels  100 us (93%)
  local copies, waits for them, and re-layouts  8.14 us (8%)
    pallas_call x1, Pallas kernels, layer_block(): pl.pallas_call(functools.partial(layer_kernel, frames, count, HEADS), out...  100 us
    transpose x1, local copies, waits for them, and re-layouts, local(): frames_out.transpose(2, 1, 0, 3).reshape(frame_count, pos_count, features)  4.07 us
    reshape x1, local copies, waits for them, and re-layouts, local(): frames_in.reshape(frame_count, blocks, steps, features)  4.07 us

profile of v2, /device:TPU:9, one launch (start us, length us, event | category | flops | bytes accessed | tf_op | source)
XLA Modules:
  0.0 108.1 jit_solution(1661316464456088267)
XLA Ops:
  0.0 4.1 %copy.17 = bf16[64,4,8,512]{3,0,1,2:T(8,128)(2,1)} copy(bf16[64,4,8,512]{3,2,1,0:T(8,128)(2,1)} %bitcast.14) | data formatting | bytes 4194304 | tf_op jit(solution)/shard_map/reshape | solution.py:576
  4.1 100.0 %shard_map.100 = bf16[2048,512]{1,0:T(8,128)(2,1)} custom-call(bf16[8,4,64,512]{3,2,1,0:T(8,128)(2,1)} %bitcast.13, f32[1,512]{1,0:T(1,128)} %bitcast.15, f32[1,512]{1,0:T(1,128)} %bitcast.16, bf16[512,512]{1,0:T(8,128)(2,1)} %wq_hbm.1, bf16[512,512]{1,0:T(8,128)(2,1)} %wk_hbm.1, bf16[512,512]{1,0:T(8,128)(2,1)} %wv_hbm.1, bf16[512,512]{1,0:T(8,128)(2,1)} %wo_hbm.1, ...), custom_call_target="tpu_custom_call" | custom-call | tf_op jit(solution)/shard_map/pallas_call | solution.py:546
  104.1 4.1 %copy.16 = bf16[64,4,8,512]{3,2,1,0:T(8,128)(2,1)} copy(bf16[64,4,8,512]{3,0,1,2:T(8,128)(2,1)} %bitcast.12) | data formatting | bytes 4194304 | tf_op jit(solution)/shard_map/transpose | solution.py:588
